TPU v7x, 32 devices: a whole 2x2x4 slice. The times are simulated.
32 devices in a mesh: section: 2 (over x), dp: 8 (over z, y), tensor: 2 (over core).
Axes of the slice: x: 2, y: 2, z: 4, core: 2. Of those that a mesh axis runs over, the one named last changes fastest.
Arguments:
- hidden: bfloat16 [2, 128, 7168], P('section', ('dp', 'tensor')), may hold values from -90 to 90
- gain: float32 [7168], replicated, may hold values from 0.5 to 1.5
- table: bfloat16 [65536, 7168], P(('dp', 'tensor')), may hold values from -4 to 4
- labels: int32 [2, 128], P('section'), may hold values from 0 to 65535
- token_weight: float32 [2, 128], P('section'), may hold values from 4 to 32
Outputs:
- grad_input: bfloat16 [2, 128, 7168], P('section', ('dp', 'tensor'))
- table_grad: bfloat16 [65536, 7168], P(('dp', 'tensor'), 'section')
All inputs are finite; a program needn't handle non-finite values.
Results may differ from a plain program's by a relative error of at most 0.0058.
Values may be sent and summed in bfloat16 or wider, within the bound.
A program may use at most 512 MiB of HBM per device.

v0:
```python
import jax
import jax.numpy as jnp
from jax import lax
from jax.sharding import PartitionSpec as P


def from_behind(block, axis, distance):
    devices = range(lax.axis_size(axis))
    route = [((i - distance) % len(devices), i) for i in devices]
    return lax.ppermute(block, axis, route)


def normalize(source_rows, gain):
    values = source_rows.astype(jnp.float32)
    inverse = lax.rsqrt(jnp.mean(values * values, axis=1, keepdims=True) + 1e-06)
    unit = values * inverse
    return (inverse, unit, (unit * gain).astype(jnp.bfloat16))


def on_device(hidden, gain, table, labels, token_weight):
    own_rows = hidden[0]
    inverse_own, unit_own, normed_own = normalize(own_rows, gain)
    gathered = lax.all_gather(own_rows, ("dp", "tensor"), axis=0, tiled=True)
    normed = normalize(gathered, gain)[2]
    logits = jnp.einsum("td,vd->tv", normed, table, preferred_element_type=jnp.float32)
    row_peak = lax.pmax(jnp.max(logits, axis=1), ("dp", "tensor"))
    row_sum = lax.psum(jnp.sum(jnp.exp(logits - row_peak[:, None]), axis=1), ("dp", "tensor"))
    log_total = row_peak + jnp.log(row_sum)
    vocab_rows = table.shape[0]
    first_entry = lax.axis_index(("dp", "tensor")) * vocab_rows
    entries = first_entry + jnp.arange(vocab_rows, dtype=jnp.int32)
    is_label = (entries[None, :] == labels[0][:, None]).astype(jnp.float32)
    logit_grad = (
        token_weight[0][:, None] * (jnp.exp(logits - log_total[:, None]) - is_label)
    ).astype(jnp.bfloat16)
    local_table = jnp.einsum("tv,td->vd", logit_grad, normed, preferred_element_type=jnp.float32)
    table_grad = lax.psum_scatter(local_table, "section", scatter_dimension=1, tiled=True).astype(
        jnp.bfloat16
    )
    normed_grad = lax.psum_scatter(
        jnp.dot(logit_grad, table, preferred_element_type=jnp.float32),
        ("dp", "tensor"),
        scatter_dimension=0,
        tiled=True,
    )
    scaled = normed_grad * gain
    section_grad = (
        inverse_own * (scaled - unit_own * jnp.mean(scaled * unit_own, axis=1, keepdims=True))
    ).astype(jnp.bfloat16)
    grad_input = from_behind(section_grad[None], "section", 1)
    return (grad_input, table_grad)


def solution(mesh):
    in_specs = (
        P("section", ("dp", "tensor"), None),
        P(),
        P(("dp", "tensor"), None),
        P("section", None),
        P("section", None),
    )
    out_specs = (P("section", ("dp", "tensor"), None), P(("dp", "tensor"), "section"))
    return jax.shard_map(
        on_device, mesh=mesh, in_specs=in_specs, out_specs=out_specs, check_vma=False
    )
```

profile of v0, /device:TPU:0, one launch (start us, length us, event | category | flops | bytes accessed | tf_op | source)
XLA Modules:
  0.0 1539.3 jit_solution(11721189287490925897)
XLA Ops:
  7.2 0.0 all-gather.3.cloned.1.call-start
  7.2 0.7 all-gather.3.cloned.1.call-update
  7.9 0.0 reduce-scatter.3.cloned.1.call-start
  8.0 45.7 %all-gather.3.cloned.1.call-done = bf16[1,128,7168]{2,1,0:T(8,128)(2,1)} async-done(((bf16[1,8,7168]{2,1,0:T(8,128)(2,1)}), bf16[1,128,7168]{2,1,0:T(8,128)(2,1)}) %all-gather.3.cloned.1.call-update) | async-done | bytes 1835024 | tf_op jit(solution)/shard_map/all_gather | solution.py:23
  53.6 1.9 fusion
  55.6 29.0 %fusion.16 = (f32[128]{0:T(128)S(1)}, f32[128,4096]{1,0:T(8,128)S(1)}) fusion(bf16[4096,7168]{1,0:T(8,128)(2,1)} %param.7, bf16[1,128,7168]{2,1,0:T(8,128)(2,1)} %all-gather.3.cloned.1.call-done, f32[7168]{0:T(1024)} %param.6, f32[128]{0:T(128)S(1)} %add_rsqrt_fusion), kind=kOutput, calls=%fused_computation.25 | convolution fusion | flops 7520387072 | bytes 62682112 | tf_op jit(solution)/shard_map/td,vd->tv/dot_general | solution.py:25
  84.7 31.3 %pmax.7 = f32[128]{0:T(128)S(1)} all-reduce(f32[128]{0:T(128)S(1)} %get-tuple-element.2), channel_id=1, replica_groups=mesh['section'=2,'dp'=8,'tensor'=2] {'dp','tensor'}, use_global_device_ids=true, to_apply=%region_3.0 | all-reduce | flops 128 | bytes 1024 | tf_op jit(solution)/shard_map/pmax | solution.py:26
  116.0 0.4 exponential_reduce_fusion
  116.4 29.5 %psum.7 = f32[128]{0:T(128)S(1)} all-reduce(f32[128]{0:T(128)S(1)} %exponential_reduce_fusion), channel_id=1, replica_groups=mesh['section'=2,'dp'=8,'tensor'=2] {'dp','tensor'}, use_global_device_ids=true, to_apply=%region_5.0 | all-reduce | flops 128 | bytes 1024 | tf_op jit(solution)/shard_map/psum | solution.py:27
  145.9 22.0 %fusion.15 = f32[128,7168]{1,0:T(8,128)} fusion(bf16[4096,7168]{1,0:T(8,128)(2,1)} %param.7, f32[128,4096]{1,0:T(8,128)S(1)} %get-tuple-element.3, s32[4096]{0:T(1024)S(1)} %iota_add_fusion, f32[128]{0:T(128)S(1)} %log_add_fusion, f32[128]{0:T(128)S(1)} %bitcast.19, s32[128]{0:T(128)S(1)} %bitcast.21), kind=kOutput, calls=%fused_computation.24 | convolution fusion | flops 7519338496 | bytes 64505344 | tf_op jit(solution)/shard_map/dot_general | solution.py:41
  168.0 0.0 reduce-scatter.3.cloned.1.call-update
  168.0 0.0 reduce-scatter.5.cloned.1.call-start
  168.0 0.7 copy-done.1
  168.7 44.0 %fusion.3 = f32[4096,7168]{1,0:T(8,128)} fusion(bf16[1,128,7168]{2,1,0:T(8,128)(2,1)} %all-gather.3.cloned.1.call-done, f32[7168]{0:T(1024)S(1)} %copy-done.1, f32[128]{0:T(128)S(1)} %add_rsqrt_fusion, f32[128,4096]{1,0:T(8,128)S(1)} %get-tuple-element.3, s32[4096]{0:T(1024)S(1)} %iota_add_fusion, f32[128]{0:T(128)S(1)} %log_add_fusion, ...), kind=kOutput, calls=%fused_computation.7 | convolution fusion | flops 7523008512 | bytes 121419776 | tf_op jit(solution)/shard_map/tv,td->vd/dot_general | solution.py:36
  212.7 0.9 copy-done
  213.6 0.2 fusion.13
  213.8 20.2 %reduce-scatter.3.cloned.1.call-done = f32[8,7168]{1,0:T(8,128)} async-done(((f32[128,7168]{1,0:T(8,128)}), f32[8,7168]{1,0:T(8,128)}) %reduce-scatter.3.cloned.1.call-update) | async-done | bytes 229392 | tf_op jit(solution)/shard_map/reduce_scatter | solution.py:40
  234.0 1.2 fusion.9
  235.2 1.1 fusion.14
  236.2 1.5 collective-permute-start
  237.8 3.3 collective-permute-done
  241.1 1262.3 %reduce-scatter.5.cloned.1.call-done = f32[4096,3584]{1,0:T(8,128)} async-done(((f32[4096,7168]{1,0:T(8,128)}), f32[4096,3584]{1,0:T(8,128)}) %reduce-scatter.5.cloned.1.call-update) | async-done | bytes 58720272 | tf_op jit(solution)/shard_map/reduce_scatter | solution.py:37
  1503.4 28.7 %convert_element_type.27 = bf16[4096,3584]{1,0:T(8,128)(2,1)} convert(f32[4096,3584]{1,0:T(8,128)} %reduce-scatter.5.cloned.1.call-done) | non-fusion elementwise | flops 14680064 | bytes 88080384 | tf_op jit(solution)/shard_map/convert_element_type | solution.py:37
  1532.1 0.6 copy.8
  (12 shorter events, 0.1 us)
Async XLA Ops:
  7.2 46.5 %all-gather.3.cloned.1.call-start = ((), (), s32[]{:S(2)}) async-start(), calls=%async_computation.4 | async-start | bytes 1949696 | tf_op jit(solution)/shard_map/all_gather | solution.py:23
  7.9 226.1 %reduce-scatter.3.cloned.1.call-start = ((), (), s32[]{:S(2)}) async-start(), calls=%async_computation.2 | async-start | bytes 3899392 | tf_op jit(solution)/shard_map/reduce_scatter | solution.py:40
  84.6 61.3 %copy-start.2 = (f32[1,128]{1,0:T(1,128)S(1)}, f32[1,128]{1,0:T(1,128)}, u32[]{:S(2)}) copy-start(f32[1,128]{1,0:T(1,128)} %param.9) | copy-start | bytes 1540
  84.6 61.3 %copy-start.3 = (s32[1,128]{1,0:T(1,128)S(1)}, s32[1,128]{1,0:T(1,128)}, u32[]{:S(2)}) copy-start(s32[1,128]{1,0:T(1,128)} %param.8) | copy-start | bytes 1540
  168.0 0.7 copy-start.1
  168.0 1335.4 %reduce-scatter.5.cloned.1.call-start = ((), (), s32[]{:S(2)}) async-start(), calls=%async_computation.3 | async-start | bytes 176160768 | tf_op jit(solution)/shard_map/reduce_scatter | solution.py:37
  212.7 0.9 copy-start
  236.2 4.9 collective-permute-start
Sparse Core Ops, SparseCore 0:
  10.3 43.3 all-gather.2
  168.1 65.8 reduce-scatter.2
  236.4 1266.9 reduce-scatter.4
where the time goes:
time: 1540 us
  waiting for transfers between devices  1330 us (86%)
  matrix products  95.1 us (6%)
  blocking collectives  60.8 us (4%)
  other arithmetic  33.5 us (2%)
    reduce_scatter x1, waiting for transfers between devices, on_device(): lax.psum_scatter(local_table, 'section', scatter_dimension=1, tiled=True)  1260 us
    all_gather x1, waiting for transfers between devices, on_device(): gathered = lax.all_gather(own_rows, ('dp', 'tensor'), axis=0, tiled=True)  45.7 us
    dot_general x1, matrix products, on_device(): jnp.einsum('tv,td->vd', logit_grad, normed, preferred_element_type=jnp.fl...  44 us
    pmax x1, blocking collectives, on_device(): row_peak = lax.pmax(jnp.max(logits, axis=1), ('dp', 'tensor'))  31.3 us
  transfers between devices with their start and end apart: 4, of which 4 were waited for; matrix products, arithmetic and copies ran while one was open for 3% of the time, Pallas kernels for 0%

commit v1 on v0

v1 whole, which is shorter than its diff:
```python
import jax
import jax.numpy as jnp
from jax import lax
from jax.sharding import PartitionSpec as P


def normalize(source_rows, gain):
    values = source_rows.astype(jnp.float32)
    inverse = lax.rsqrt(jnp.mean(values * values, axis=1, keepdims=True) + 1e-06)
    unit = values * inverse
    return (inverse, unit, (unit * gain).astype(jnp.bfloat16))


def on_device(hidden, gain, table, labels, token_weight):
    section = lax.axis_index("section")
    tokens = labels.shape[1]
    vocab_rows, width = table.shape
    half = width // 2
    normed_own = normalize(hidden[0], gain)[2]
    normed = lax.all_gather(normed_own, ("section", "dp", "tensor"), axis=0, tiled=True)
    other_rows = lax.ppermute(hidden[0], "section", [(0, 1), (1, 0)])
    labels_all = lax.all_gather(labels[0], "section", axis=0, tiled=True)
    weight_all = lax.all_gather(token_weight[0], "section", axis=0, tiled=True)
    logits = jnp.einsum("td,vd->tv", normed, table, preferred_element_type=jnp.float32)
    peak = jnp.max(logits, axis=1)
    part = jnp.sum(jnp.exp(logits - peak[:, None]), axis=1)
    stats = lax.all_gather(jnp.stack([peak, part]), ("dp", "tensor"), axis=0)
    row_peak = jnp.max(stats[:, 0], axis=0)
    row_sum = jnp.sum(stats[:, 1] * jnp.exp(stats[:, 0] - row_peak[None]), axis=0)
    log_total = row_peak + jnp.log(row_sum)
    first_entry = lax.axis_index(("dp", "tensor")) * vocab_rows
    entries = first_entry + jnp.arange(vocab_rows, dtype=jnp.int32)
    is_label = (entries[None, :] == labels_all[:, None]).astype(jnp.float32)
    logit_grad = (
        weight_all[:, None] * (jnp.exp(logits - log_total[:, None]) - is_label)
    ).astype(jnp.bfloat16)
    other_grad = lax.dynamic_slice_in_dim(logit_grad, (1 - section) * tokens, tokens, axis=0)
    normed_grad = lax.psum_scatter(
        jnp.dot(other_grad, table, preferred_element_type=jnp.float32),
        ("dp", "tensor"),
        scatter_dimension=0,
        tiled=True,
    )
    own_columns = lax.dynamic_slice_in_dim(normed, section * half, half, axis=1)
    table_grad = jnp.einsum(
        "tv,td->vd", logit_grad, own_columns, preferred_element_type=jnp.float32
    ).astype(jnp.bfloat16)
    inverse, unit, _ = normalize(other_rows, gain)
    scaled = normed_grad * gain
    section_grad = (
        inverse * (scaled - unit * jnp.mean(scaled * unit, axis=1, keepdims=True))
    ).astype(jnp.bfloat16)
    return (section_grad[None], table_grad)


def solution(mesh):
    in_specs = (
        P("section", ("dp", "tensor"), None),
        P(),
        P(("dp", "tensor"), None),
        P("section", None),
        P("section", None),
    )
    out_specs = (P("section", ("dp", "tensor"), None), P(("dp", "tensor"), "section"))
    return jax.shard_map(
        on_device, mesh=mesh, in_specs=in_specs, out_specs=out_specs, check_vma=False
    )
```

time: 1540 us -> 225 us (0.15)
  waiting for transfers between devices: 1330 us -> 105 us
  blocking collectives: 60.8 us -> 29.9 us
  matrix products: 95.1 us -> 64.3 us
  other arithmetic: 33.5 us -> 10.3 us
    reduce_scatter x2 -> x1, waiting for transfers between devices: 1280 us -> 45.1 us  [on_device(): lax.psum_scatter(jnp.dot(other_grad, table, preferred_element_type=jnp.fl...]
    pmax x1 -> x0, blocking collectives: 31.3 us -> none  [on_device(): row_peak = lax.pmax(jnp.max(logits, axis=1), ('dp', 'tensor'))]
    all_gather x0 -> x3, blocking collectives: none -> 29.9 us  [the longest x1 20.2 us: on_device(): stats = lax.all_gather(jnp.stack([peak, part]), ('dp', 'tensor'), axis=0)]
    dot_general x2, matrix products: 66 us -> 36.3 us  [the longest x1 22 us: on_device(): jnp.dot(other_grad, table, preferred_element_type=jnp.float32)]
    psum x1 -> x0, blocking collectives: 29.5 us -> none  [on_device(): lax.psum(jnp.sum(jnp.exp(logits - row_peak[:, None]), axis=1), ('dp', 'te...]
    convert_element_type x1 -> x2, other arithmetic: 28.7 us -> 3.02 us  [the longest x1 1.66 us: normalize(): return (inverse, unit, (unit * gain).astype(jnp.bfloat16))]
  transfers between devices with their start and end apart: 4 -> 3, of which waited for: 4 -> 3; matrix products, arithmetic and copies ran while one was open for 3% -> 6% of each run, Pallas kernels for 0% -> 0%
where the time goes in v1:
time: 225 us; the launch traced here: 224 us
  waiting for transfers between devices  105 us (47%)
  matrix products  64.3 us (29%)
  blocking collectives  29.9 us (13%)
  between operations  14.1 us (6%)
  other arithmetic  10.3 us (5%)
    all_gather x1, waiting for transfers between devices, on_device(): lax.all_gather(normed_own, ('section', 'dp', 'tensor'), axis=0, tiled=True)  55 us
    reduce_scatter x1, waiting for transfers between devices, on_device(): lax.psum_scatter(jnp.dot(other_grad, table, preferred_element_type=jnp.fl...  45.1 us
    dot_general x1, matrix products, on_device(): jnp.einsum('td,vd->tv', normed, table, preferred_element_type=jnp.float32)  28 us
    dot_general x1, matrix products, on_device(): jnp.dot(other_grad, table, preferred_element_type=jnp.float32)  22 us
    all_gather x1, blocking collectives, on_device(): stats = lax.all_gather(jnp.stack([peak, part]), ('dp', 'tensor'), axis=0)  20.2 us
    dot_general x1, matrix products, on_device(): jnp.einsum('tv,td->vd', logit_grad, own_columns, preferred_element_type=j...  14.4 us
    all_gather x1, blocking collectives, on_device(): labels_all = lax.all_gather(labels[0], 'section', axis=0, tiled=True)  5.31 us
    ppermute x1, waiting for transfers between devices, on_device(): other_rows = lax.ppermute(hidden[0], 'section', [(0, 1), (1, 0)])  4.82 us
  transfers between devices with their start and end apart: 3, of which 3 were waited for; matrix products, arithmetic and copies ran while one was open for 6% of the time, Pallas kernels for 0%

profile of v1, /device:TPU:0, one launch (start us, length us, event | category | flops | bytes accessed | tf_op | source)
XLA Modules:
  0.0 224.2 jit_solution(2610202502424764168)
XLA Ops:
  7.2 0.0 all-gather.6.cloned.1.call-start
  7.2 1.1 fusion.10
  8.3 1.7 fusion.12
  10.0 0.0 all-gather.6.cloned.1.call-update
  10.0 0.0 reduce-scatter.2.cloned.1.call-start
  10.0 5.3 %all-gather.2 = s32[1,256]{1,0:T(1,128)S(1)} all-gather(s32[1,128]{1,0:T(1,128)} %param.8), channel_id=4, replica_groups=mesh['section'=2,'dp'=8,'tensor'=2] {'section'}, dimensions={1}, use_global_device_ids=true | all-gather | bytes 1536 | tf_op jit(solution)/shard_map/all_gather | solution.py:22
  15.3 4.3 %all-gather = f32[1,256]{1,0:T(1,128)S(1)} all-gather(f32[1,128]{1,0:T(1,128)} %param.9), channel_id=2, replica_groups=mesh['section'=2,'dp'=8,'tensor'=2] {'section'}, dimensions={1}, use_global_device_ids=true | all-gather | bytes 1536 | tf_op jit(solution)/shard_map/all_gather | solution.py:23
  19.7 55.0 %all-gather.6.cloned.1.call-done = bf16[256,7168]{1,0:T(8,128)(2,1)} async-done(((bf16[8,7168]{1,0:T(8,128)(2,1)}), bf16[256,7168]{1,0:T(8,128)(2,1)}) %all-gather.6.cloned.1.call-update) | async-done | bytes 3670032 | tf_op jit(solution)/shard_map/all_gather | solution.py:20
  74.7 28.0 %fusion.20 = (f32[256]{0:T(256)S(1)}, f32[256,4096]{1,0:T(8,128)}) fusion(bf16[256,7168]{1,0:T(8,128)(2,1)} %all-gather.6.cloned.1.call-done, bf16[4096,7168]{1,0:T(8,128)(2,1)} %param.7), kind=kOutput, calls=%fused_computation.36 | convolution fusion | flops 15033434112 | bytes 66585600 | tf_op jit(solution)/shard_map/td,vd->tv/dot_general | solution.py:24
  102.6 3.0 %exponential_reduce_fusion = f32[256]{0:T(256)S(1)} fusion(f32[256,4096]{1,0:T(8,128)} %get-tuple-element.6, f32[256]{0:T(256)S(1)} %get-tuple-element.5), kind=kLoop, calls=%fused_computation.2 | loop fusion | flops 2096896 | bytes 4196352 | tf_op jit(solution)/shard_map/reduce_sum | solution.py:26
  105.7 20.2 %all-gather.3 = f32[16,2,256]{2,1,0:T(2,128)S(1)} all-gather(f32[1,2,256]{2,1,0:T(2,128)S(1)} %maximum_bitcast_fusion), channel_id=3, replica_groups=mesh['section'=2,'dp'=8,'tensor'=2] {'dp','tensor'}, dimensions={0}, use_global_device_ids=true | all-gather | bytes 34816 | tf_op jit(solution)/shard_map/all_gather | solution.py:27
  126.0 0.0 copy-done
  126.0 1.4 multiply_convert_fusion
  127.4 0.0 copy-start.1
  127.4 22.0 %fusion.1 = f32[128,7168]{1,0:T(8,128)} fusion(bf16[4096,7168]{1,0:T(8,128)(2,1)} %param.7, bf16[256,4096]{1,0:T(8,128)(2,1)S(1)} %multiply_convert_fusion, s32[]{:T(128)S(6)} %select_n.6), kind=kOutput, calls=%fused_computation.4 | convolution fusion | flops 7516192768 | bytes 63438852 | tf_op jit(solution)/shard_map/dot_general | solution.py:39
  149.3 0.0 reduce-scatter.2.cloned.1.call-update
  149.4 0.0 copy-done.1
  149.4 0.6 collective-permute-start
  150.0 4.8 %collective-permute-done = bf16[8,7168]{1,0:T(8,128)(2,1)S(1)} collective-permute-done((bf16[8,7168]{1,0:T(8,128)(2,1)S(1)}, bf16[8,7168]{1,0:T(8,128)(2,1)S(1)}, u32[]{:S(2)}, u32[]{:S(2)}) %collective-permute-start) | collective-permute-done | bytes 114720 | tf_op jit(solution)/shard_map/ppermute | solution.py:21
  154.8 0.2 fusion.9
  155.0 14.4 %convolution_convert_fusion = bf16[4096,3584]{1,0:T(8,128)(2,1)} fusion(bf16[256,4096]{1,0:T(8,128)(2,1)S(1)} %multiply_convert_fusion, bf16[256,7168]{1,0:T(8,128)(2,1)} %all-gather.6.cloned.1.call-done, s32[]{:T(128)S(6)} %select_n.7), kind=kOutput, calls=%fused_computation | convolution fusion | flops 7530872832 | bytes 33292292 | tf_op jit(solution)/shard_map/tv,td->vd/dot_general | solution.py:45
  169.4 45.1 %reduce-scatter.2.cloned.1.call-done = f32[8,7168]{1,0:T(8,128)} async-done(((f32[128,7168]{1,0:T(8,128)}), f32[8,7168]{1,0:T(8,128)}) %reduce-scatter.2.cloned.1.call-update) | async-done | bytes 229392 | tf_op jit(solution)/shard_map/reduce_scatter | solution.py:38
  214.5 1.2 fusion.5
  215.6 1.7 fusion.13
  (11 shorter events, 0.1 us)
Async XLA Ops:
  7.2 67.5 %all-gather.6.cloned.1.call-start = ((), (), s32[]{:S(2)}) async-start(), calls=%async_computation.1 | async-start | bytes 3784704 | tf_op jit(solution)/shard_map/all_gather | solution.py:20
  10.0 204.5 %reduce-scatter.2.cloned.1.call-start = ((), (), s32[]{:S(2)}) async-start(), calls=%async_computation.2 | async-start | bytes 3899392 | tf_op jit(solution)/shard_map/reduce_scatter | solution.py:38
  102.6 23.4 %copy-start = (f32[256,4096]{1,0:T(8,128)S(1)}, f32[256,4096]{1,0:T(8,128)}, u32[]{:S(2)}) copy-start(f32[256,4096]{1,0:T(8,128)} %get-tuple-element.6) | copy-start | bytes 12582916
  127.4 22.0 %copy-start.1 = (bf16[1,8,7168]{2,1,0:T(8,128)(2,1)S(1)}, bf16[1,8,7168]{2,1,0:T(8,128)(2,1)}, u32[]{:S(2)}) copy-start(bf16[1,8,7168]{2,1,0:T(8,128)(2,1)} %param.5) | copy-start | bytes 344068
  149.4 5.5 %collective-permute-start = (bf16[8,7168]{1,0:T(8,128)(2,1)S(1)}, bf16[8,7168]{1,0:T(8,128)(2,1)S(1)}, u32[]{:S(2)}, u32[]{:S(2)}) collective-permute-start(bf16[8,7168]{1,0:T(8,128)(2,1)S(1)} %bitcast.27), channel_id=1, source_target_pairs={{0,16},{16,0},{1,17},{17,1},{2,18},{18,2},{3,19},{19,3},{4,20},{20... | collective-permute-start | bytes 344072 | tf_op jit(solution)/shard_map/ppermute | solution.py:21
  155.0 59.5 %copy-start.2 = (f32[7168]{0:T(1024)S(1)}, f32[7168]{0:T(1024)}, u32[]{:S(2)}) copy-start(f32[7168]{0:T(1024)} %param.6) | copy-start | bytes 86020
Sparse Core Ops, SparseCore 0:
  11.4 63.1 all-gather.5
  149.5 64.9 reduce-scatter.1

commit v2 on v1

--- a/solution.py
+++ b/solution.py
@@ -1,6 +1,8 @@
 import jax
 import jax.numpy as jnp
 from jax import lax
+from jax.experimental import pallas as pl
+from jax.experimental.pallas import tpu as pltpu
 from jax.sharding import PartitionSpec as P
 
 
@@ -11,7 +13,389 @@
     return (inverse, unit, (unit * gain).astype(jnp.bfloat16))
 
 
-def on_device(hidden, gain, table, labels, token_weight):
+MESH = pl.DeviceIdType.MESH
+PAIR = 1024
+SLAB = 512
+SLOTS = 4
+TILE = 512
+
+
+def fused_kernel(
+    hidden_ref, gain_ref, table_ref, marks_ref,
+    grad_out, rows_out, sum_out,
+    rows, both, other_marks, ring, logits, grad_t, grad_o, stat_out, stat_in,
+    mine, sent, got, y_part, y_sent, y_got, z_sent, z_got, final, cross,
+    ring_sem, out_sem, pair_sem, mark_sem, z_sem, near_sem, sib_sem, stat_sem,
+    back_sem, last_sem,
+):
+    x = lax.axis_index("section")
+    dp = lax.axis_index("dp")
+    core = lax.axis_index("tensor")
+    z, y = dp // 2, dp % 2
+    pairs = table_ref.shape[1] // PAIR
+    vocab = table_ref.shape[0]
+    half = rows_out.shape[4]
+    tiles = vocab // TILE
+
+    sibling = {"tensor": 1 - core}
+    across = {"section": 1 - x}
+    beside = {"dp": z * 2 + (1 - y)}
+
+    def along(step):
+        return {"dp": ((z + step) % 4) * 2 + y}
+
+    def load(pair):
+        return pltpu.make_async_copy(
+            table_ref.at[:, pl.ds(pl.multiple_of(pair * PAIR, PAIR), PAIR)],
+            ring.at[pair % SLOTS],
+            ring_sem.at[pair % SLOTS],
+        )
+
+    for pair in range(SLOTS):
+        load(pair).start()
+
+    def remote(src, dst, send, recv, device):
+        return pltpu.make_async_remote_copy(
+            src_ref=src, dst_ref=dst, send_sem=send, recv_sem=recv,
+            device_id=device, device_id_type=MESH,
+        )
+
+    barrier = pltpu.get_barrier_semaphore()
+    peers = [sibling, across, beside, along(1), along(2), along(3)]
+    for peer in peers:
+        pl.semaphore_signal(barrier, inc=1, device_id=peer, device_id_type=MESH)
+
+    values = hidden_ref[...].astype(jnp.float32)
+    inverse = lax.rsqrt(jnp.mean(values * values, axis=1, keepdims=True) + 1e-06)
+    normed = (values * inverse * gain_ref[...]).astype(jnp.bfloat16)
+    both[core] = normed.astype(jnp.float32)
+    pl.semaphore_wait(barrier, len(peers))
+
+    pair_copy = remote(both.at[core], both.at[core], pair_sem.at[0], pair_sem.at[1], sibling)
+    pair_copy.start()
+    mark_copy = remote(marks_ref, other_marks, mark_sem.at[0], mark_sem.at[1], across)
+    mark_copy.start()
+    pair_copy.wait()
+
+    def columns(step):
+        return pl.ds(pl.multiple_of((2 * step + core) * SLAB, SLAB), SLAB)
+
+    def z_copy(step, d):
+        block = rows.at[0, z, y, :, columns(step)]
+        return remote(block, block, z_sem.at[0, d - 1, step], z_sem.at[1, d - 1, step], along(d))
+
+    first = (
+        (1 - core) * (1 - x) + core * x,
+        z * 2 + (1 - core) * y + core * (1 - y),
+        core,
+    )
+    second = (
+        core * (1 - x) + (1 - core) * x,
+        z * 2 + core * y + (1 - core) * (1 - y),
+        core,
+    )
+    far_y = (1 - core) * y + core * (1 - y)
+
+    def near_copy(step, kind):
+        cols = columns(step)
+        if kind == 0:
+            src, dst, device = rows.at[0, :, y, :, cols], rows.at[1 - core, :, y, :, cols], first
+        elif kind == 1:
+            src, dst, device = rows.at[0, :, y, :, cols], rows.at[core, :, y, :, cols], second
+        else:
+            src = rows.at[1 - core, :, far_y, :, cols]
+            dst, device = rows.at[1, :, far_y, :, cols], second
+        return remote(src, dst, near_sem.at[0, kind, step], near_sem.at[1, kind, step], device)
+
+    def sib_copy(step):
+        block = rows.at[:, :, :, :, columns(step)]
+        return remote(block, block, sib_sem.at[0, step], sib_sem.at[1, step], sibling)
+
+    @pl.loop(0, pairs)
+    def _(step):
+        rows[0, z, y, :, columns(step)] = (
+            both[:, :, columns(step)].reshape(16, SLAB).astype(jnp.bfloat16)
+        )
+        for d in (1, 2, 3):
+            z_copy(step, d).start()
+
+    @pl.loop(0, pairs + 3)
+    def _(i):
+        @pl.when(i < pairs)
+        def _():
+            for d in (1, 2, 3):
+                z_copy(i, d).wait_recv()
+            near_copy(i, 0).start()
+            near_copy(i, 1).start()
+
+        @pl.when((i >= 1) & (i < pairs + 1))
+        def _():
+            near_copy(i - 1, 0).wait_recv()
+            near_copy(i - 1, 2).start()
+
+        @pl.when((i >= 2) & (i < pairs + 2))
+        def _():
+            near_copy(i - 2, 1).wait_recv()
+            near_copy(i - 2, 2).wait_recv()
+            sib_copy(i - 2).start()
+
+        @pl.when(i >= 3)
+        def _():
+            p = i - 3
+            sib_copy(p).wait_recv()
+            load(p).wait()
+            slot = p % SLOTS
+            right = rows[:, :, :, :, pl.ds(pl.multiple_of(p * PAIR, PAIR), PAIR)].reshape(-1, PAIR)
+
+            def product(t):
+                at = pl.ds(pl.multiple_of(t * TILE, TILE), TILE)
+                return at, lax.dot_general(
+                    ring[slot, at, :], right, (((1,), (1,)), ((), ())),
+                    preferred_element_type=jnp.float32,
+                )
+
+            @pl.when(p == 0)
+            def _():
+                @pl.loop(0, tiles)
+                def _(t):
+                    at, term = product(t)
+                    logits[at, :] = term
+
+            @pl.when(p > 0)
+            def _():
+                @pl.loop(0, tiles)
+                def _(t):
+                    at, term = product(t)
+                    logits[at, :] += term
+
+            @pl.when(p + SLOTS < pairs)
+            def _():
+                load(p + SLOTS).start()
+
+    rows_copy = pltpu.make_async_copy(
+        rows.at[:, :, :, :, pl.ds(pl.multiple_of(x * half, 128), half)], rows_out, out_sem.at[0]
+    )
+    rows_copy.start()
+
+    count = logits.shape[1]
+
+    def top(t, best):
+        at = pl.ds(pl.multiple_of(t * TILE, TILE), TILE)
+        return jnp.maximum(best, jnp.max(logits[at, :].reshape(TILE // 8, 8, count), axis=0))
+
+    best = lax.fori_loop(0, tiles, top, jnp.full((8, count), -jnp.inf, jnp.float32))
+    peak = jnp.max(best, axis=0, keepdims=True)
+
+    def accumulate(t, total):
+        at = pl.ds(pl.multiple_of(t * TILE, TILE), TILE)
+        e = jnp.exp(logits[at, :] - peak)
+        logits[at, :] = e
+        return total + jnp.sum(e.reshape(TILE // 8, 8, count), axis=0)
+
+    part = lax.fori_loop(0, tiles, accumulate, jnp.zeros((8, count), jnp.float32))
+    part = jnp.sum(part, axis=0, keepdims=True)
+
+    def stat_copy(stage, slot, device):
+        return remote(
+            stat_out.at[stage], stat_in.at[slot], stat_sem.at[0, slot], stat_sem.at[1, slot], device
+        )
+
+    row_peak, row_sum = peak, part
+    slot = 0
+    stat_copies = []
+    for stage, devices in enumerate(([sibling], [beside], [along(1), along(2), along(3)])):
+        stat_out[stage, 0:8] = jnp.broadcast_to(row_peak, (8, count))
+        stat_out[stage, 8:16] = jnp.broadcast_to(row_sum, (8, count))
+        copies = [stat_copy(stage, slot + i, device) for i, device in enumerate(devices)]
+        for copy in copies:
+            copy.start()
+        for i, copy in enumerate(copies):
+            copy.wait_recv()
+            got_peak, got_sum = stat_in[slot + i, 0:1], stat_in[slot + i, 8:9]
+            new_peak = jnp.maximum(row_peak, got_peak)
+            row_sum = row_sum * jnp.exp(row_peak - new_peak) + got_sum * jnp.exp(got_peak - new_peak)
+            row_peak = new_peak
+        slot += len(devices)
+        stat_copies += copies
+    factor = jnp.exp(peak - row_peak - jnp.log(row_sum))
+
+    mark_copy.wait()
+    label = jnp.concatenate([marks_ref[0:1], other_marks[0:1]], axis=1).astype(jnp.int32)
+    weight = jnp.concatenate([marks_ref[1:2], other_marks[1:2]], axis=1)
+    label = label - (dp * 2 + core) * vocab
+
+    @pl.loop(0, tiles)
+    def _(t):
+        at = pl.ds(pl.multiple_of(t * TILE, TILE), TILE)
+        entry = lax.broadcasted_iota(jnp.int32, (TILE, count), 0) + t * TILE
+        hit = jnp.where(entry == label, 1.0, 0.0)
+        g = weight * (logits[at, :] * factor - hit)
+        grad_t[at, :] = g.astype(jnp.bfloat16)
+        grad_o[:, at] = g[:, count // 2 :].T.astype(jnp.bfloat16)
+
+    grad_copy = pltpu.make_async_copy(grad_t, grad_out, out_sem.at[1])
+    grad_copy.start()
+
+    def give(i):
+        return remote(sent.at[i], got.at[i], back_sem.at[0, 0, i], back_sem.at[1, 0, i], sibling)
+
+    def give_y(i):
+        return remote(y_sent.at[i], y_got.at[i], back_sem.at[0, 1, i], back_sem.at[1, 1, i], beside)
+
+    def give_z(i, d):
+        return remote(
+            z_sent.at[i, (z + d) % 4], z_got.at[i, d - 1],
+            back_sem.at[0, 1 + d, i], back_sem.at[1, 1 + d, i], along(d),
+        )
+
+    @pl.loop(0, pairs + 3)
+    def _(i):
+        @pl.when(i < pairs)
+        def _():
+            p = pairs - 1 - i
+
+            @pl.when(p < pairs - SLOTS)
+            def _():
+                load(p).wait()
+
+            slot = p % SLOTS
+
+            def dot(which):
+                cols = pl.ds(pl.multiple_of(which * SLAB, SLAB), SLAB)
+                return jnp.dot(grad_o[...], ring[slot, :, cols], preferred_element_type=jnp.float32)
+
+            sent[i] = dot(1 - core).reshape(4, 2, 16, SLAB)
+            give(i).start()
+            mine[i] = dot(core).reshape(4, 2, 16, SLAB)
+
+            @pl.when(p >= SLOTS)
+            def _():
+                load(p - SLOTS).start()
+
+        @pl.when((i >= 1) & (i < pairs + 1))
+        def _():
+            j = i - 1
+            give(j).wait_recv()
+            y_sent[j] = (mine[j, :, 1 - y] + got[j, :, 1 - y]).astype(jnp.bfloat16)
+            give_y(j).start()
+            y_part[j] = mine[j, :, y] + got[j, :, y]
+
+        @pl.when((i >= 2) & (i < pairs + 2))
+        def _():
+            j = i - 2
+            give_y(j).wait_recv()
+            total = y_part[j] + y_got[j].astype(jnp.float32)
+            y_part[j] = total
+            z_sent[j] = total.astype(jnp.bfloat16)
+            for d in (1, 2, 3):
+                give_z(j, d).start()
+
+        @pl.when(i >= 3)
+        def _():
+            j = i - 3
+            total = y_part[j, z]
+            for d in (1, 2, 3):
+                give_z(j, d).wait_recv()
+                total = total + z_got[j, d - 1].astype(jnp.float32)
+            final[0, pairs - 1 - j] = total[0:8]
+            final[1, pairs - 1 - j] = total[8:16]
+
+    last = remote(final.at[1 - core], cross, last_sem.at[0], last_sem.at[1], sibling)
+    last.start()
+    last.wait()
+    sum_out[core] = final[core]
+    sum_out[1 - core] = cross[...]
+
+    for copy in stat_copies:
+        copy.wait_send()
+
+    @pl.loop(0, pairs)
+    def _(i):
+        for d in (1, 2, 3):
+            z_copy(i, d).wait_send()
+            give_z(i, d).wait_send()
+        for kind in (0, 1, 2):
+            near_copy(i, kind).wait_send()
+        sib_copy(i).wait_send()
+        give(i).wait_send()
+        give_y(i).wait_send()
+
+    rows_copy.wait()
+    grad_copy.wait()
+
+
+def fused_plan(hidden, gain, table, labels, token_weight):
+    section = lax.axis_index("section")
+    tokens = labels.shape[1]
+    vocab, width = table.shape
+    half, pairs = width // 2, width // PAIR
+    own = hidden.shape[1]
+    other_rows = lax.ppermute(hidden[0], "section", [(0, 1), (1, 0)])
+    marks = jnp.concatenate(
+        [labels.astype(jnp.float32), token_weight, jnp.zeros((6, tokens), jnp.float32)], axis=0
+    )
+    f32, b16, sem = jnp.float32, jnp.bfloat16, pltpu.SemaphoreType.DMA
+    vmem, anywhere = pl.BlockSpec(memory_space=pltpu.VMEM), pl.BlockSpec(memory_space=pl.ANY)
+    grad_t, rows, sums = pl.pallas_call(
+        fused_kernel,
+        out_shape=(
+            jax.ShapeDtypeStruct((vocab, 2 * tokens), b16),
+            jax.ShapeDtypeStruct((2, 4, 2, 16, half), b16),
+            jax.ShapeDtypeStruct((2, pairs, own, SLAB), f32),
+        ),
+        in_specs=[vmem, vmem, anywhere, vmem],
+        out_specs=(anywhere, anywhere, vmem),
+        scratch_shapes=[
+            pltpu.VMEM((2, 4, 2, 16, width), b16),
+            pltpu.VMEM((2, own, width), f32),
+            pltpu.VMEM((8, tokens), f32),
+            pltpu.VMEM((SLOTS, vocab, PAIR), b16),
+            pltpu.VMEM((vocab, 2 * tokens), f32),
+            pltpu.VMEM((vocab, 2 * tokens), b16),
+            pltpu.VMEM((tokens, vocab), b16),
+            pltpu.VMEM((3, 16, 2 * tokens), f32),
+            pltpu.VMEM((5, 16, 2 * tokens), f32),
+            pltpu.VMEM((pairs, 4, 2, 16, SLAB), f32),
+            pltpu.VMEM((pairs, 4, 2, 16, SLAB), f32),
+            pltpu.VMEM((pairs, 4, 2, 16, SLAB), f32),
+            pltpu.VMEM((pairs, 4, 16, SLAB), f32),
+            pltpu.VMEM((pairs, 4, 16, SLAB), b16),
+            pltpu.VMEM((pairs, 4, 16, SLAB), b16),
+            pltpu.VMEM((pairs, 4, 16, SLAB), b16),
+            pltpu.VMEM((pairs, 3, 16, SLAB), b16),
+            pltpu.VMEM((2, pairs, own, SLAB), f32),
+            pltpu.VMEM((pairs, own, SLAB), f32),
+            sem((SLOTS,)),
+            sem((2,)),
+            sem((2,)),
+            sem((2,)),
+            sem((2, 3, pairs)),
+            sem((2, 3, pairs)),
+            sem((2, pairs)),
+            sem((2, 5)),
+            sem((2, 5, pairs)),
+            sem((2,)),
+        ],
+        compiler_params=pltpu.CompilerParams(
+            collective_id=0, has_side_effects=True, vmem_limit_bytes=60 * 2**20
+        ),
+        cost_estimate=pl.CostEstimate(
+            flops=6 * tokens * vocab * width, bytes_accessed=3 * vocab * width, transcendentals=0
+        ),
+    )(hidden[0], gain[None], table, marks)
+    table_grad = jnp.einsum(
+        "vt,td->vd", grad_t, rows.reshape(2 * tokens, half), preferred_element_type=f32
+    ).astype(b16)
+    normed_grad = jnp.transpose(sums, (2, 1, 0, 3)).reshape(own, width)
+    inverse, unit, _ = normalize(other_rows, gain)
+    scaled = normed_grad * gain
+    section_grad = (
+        inverse * (scaled - unit * jnp.mean(scaled * unit, axis=1, keepdims=True))
+    ).astype(b16)
+    return (section_grad[None], table_grad)
+
+
+def plain_plan(hidden, gain, table, labels, token_weight):
     section = lax.axis_index("section")
     tokens = labels.shape[1]
     vocab_rows, width = table.shape
@@ -62,6 +446,18 @@
         P("section", None),
     )
     out_specs = (P("section", ("dp", "tensor"), None), P(("dp", "tensor"), "section"))
+    sizes = (mesh.shape["section"], mesh.shape["dp"], mesh.shape["tensor"])
+
+    def on_device(hidden, gain, table, labels, token_weight):
+        fits = (
+            sizes == (2, 8, 2)
+            and hidden.shape[1] == 8
+            and table.shape[0] == 4096
+            and table.shape[1] % (2 * PAIR) == PAIR
+        )
+        plan = fused_plan if fits else plain_plan
+        return plan(hidden, gain, table, labels, token_weight)
+
     return jax.shard_map(
         on_device, mesh=mesh, in_specs=in_specs, out_specs=out_specs, check_vma=False
     )

time: 225 us -> 109 us (0.48)
  waiting for transfers between devices: 105 us -> 0.01 us
  Pallas kernels: 0 us -> 86.7 us
  matrix products: 64.3 us -> 14.9 us
  blocking collectives: 29.9 us -> 0 us
  between operations: 14.1 us -> 0.67 us
  other arithmetic: 10.3 us -> 3.17 us
  starting transfers between devices: 0.71 us -> 3 us
    pallas_call x0 -> x1, Pallas kernels: none -> 86.7 us  [fused_plan(): pl.pallas_call(fused_kernel, out_shape=(jax.ShapeDtypeStruct((vocab, 2 *...]
    all_gather x1 -> x0, waiting for transfers between devices: 55 us -> none  [on_device(): lax.all_gather(normed_own, ('section', 'dp', 'tensor'), axis=0, tiled=True)]
    dot_general x3 -> x1, matrix products: 64.3 us -> 14.9 us  [fused_plan(): jnp.einsum('vt,td->vd', grad_t, rows.reshape(2 * tokens, half), preferred...]
    reduce_scatter x1 -> x0, waiting for transfers between devices: 45.1 us -> none  [on_device(): lax.psum_scatter(jnp.dot(other_grad, table, preferred_element_type=jnp.fl...]
    all_gather x3 -> x0, blocking collectives: 29.9 us -> none  [the longest x1 20.2 us: on_device(): stats = lax.all_gather(jnp.stack([peak, part]), ('dp', 'tensor'), axis=0)]
    ppermute x1, waiting for transfers between devices: 4.82 us -> 0.01 us  [fused_plan(): other_rows = lax.ppermute(hidden[0], 'section', [(0, 1), (1, 0)])]
    reduce_sum x3 -> x1, other arithmetic: 4.25 us -> 0.25 us  [fused_plan(): jnp.mean(scaled * unit, axis=1, keepdims=True)]
    ppermute x1, starting transfers between devices: 0.63 us -> 3 us  [fused_plan(): other_rows = lax.ppermute(hidden[0], 'section', [(0, 1), (1, 0)])]
  transfers between devices with their start and end apart: 3 -> 1, of which waited for: 3 -> 0; matrix products, arithmetic and copies ran while one was open for 6% -> 16% of each run, Pallas kernels for 0% -> 80%
where the time goes in v2:
time: 109 us
  Pallas kernels  86.7 us (80%)
  matrix products  14.9 us (14%)
  other arithmetic  3.17 us (3%)
  starting transfers between devices  3 us (3%)
    pallas_call x1, Pallas kernels, fused_plan(): pl.pallas_call(fused_kernel, out_shape=(jax.ShapeDtypeStruct((vocab, 2 *...  86.7 us
    dot_general x1, matrix products, fused_plan(): jnp.einsum('vt,td->vd', grad_t, rows.reshape(2 * tokens, half), preferred...  14.9 us
    ppermute x1, starting transfers between devices, fused_plan(): other_rows = lax.ppermute(hidden[0], 'section', [(0, 1), (1, 0)])  3 us
  transfers between devices with their start and end apart: 1, of which 0 were waited for; matrix products, arithmetic and copies ran while one was open for 16% of the time, Pallas kernels for 80%

profile of v2, /device:TPU:0, one launch (start us, length us, event | category | flops | bytes accessed | tf_op | source)
XLA Modules:
  0.0 108.5 jit_solution(17432412549737762773)
XLA Ops:
  0.6 3.0 %collective-permute-start = (bf16[8,7168]{1,0:T(8,128)(2,1)}, bf16[8,7168]{1,0:T(8,128)(2,1)S(1)}, u32[]{:S(2)}, u32[]{:S(2)}) collective-permute-start(bf16[8,7168]{1,0:T(8,128)(2,1)} %bitcast.14), channel_id=1, source_target_pairs={{0,16},{16,0},{1,17},{17,1},{2,18},{18,2},{3,19},{19,3},{4,20},{20... | collective-permute-start | bytes 344072 | tf_op jit(solution)/shard_map/ppermute | solution.py:333
  3.6 0.7 convert_element_type.13
  4.3 0.1 pad.2.clone
  4.4 1.3 %maximum_maximum_fusion.marks_ref = f32[8,128]{1,0:T(8,128)} fusion(f32[1,128]{1,0:T(1,128)} %param.9, f32[1,128]{1,0:T(1,128)S(1)} %convert_element_type.13, f32[8]{0:T(128)S(1)} %pad.2.clone), kind=kLoop, calls=%fused_computation.11 | loop fusion | flops 2048 | bytes 5152 | tf_op jit(solution)/shard_map/concatenate | solution.py:334
  5.7 86.7 %shard_map.68 = (bf16[4096,256]{1,0:T(8,128)(2,1)}, bf16[2,4,2,16,3584]{4,3,2,1,0:T(8,128)(2,1)}, f32[2,7,8,512]{3,2,1,0:T(8,128)}) custom-call(bf16[8,7168]{1,0:T(8,128)(2,1)} %bitcast.15, f32[1,7168]{1,0:T(1,128)} %bitcast.13, bf16[4096,7168]{1,0:T(8,128)(2,1)} %table_ref.1, f32[8,128]{1,0:T(8,128)} %maximum_maximum_fusion.marks_ref), custom_call_target="tpu_custom_call" | custom-call | flops 22548578304 | bytes 88080384 | tf_op jit(solution)/shard_map/pallas_call | solution.py:339
  92.4 0.0 copy-start
  92.4 0.0 copy-start.1
  92.4 14.9 %convolution_convert_fusion = bf16[4096,3584]{1,0:T(8,128)(2,1)} fusion(bf16[4096,256]{1,0:T(8,128)(2,1)} %get-tuple-element.6, bf16[256,3584]{1,0:T(8,128)(2,1)} %bitcast.11), kind=kOutput, calls=%fused_computation | convolution fusion | flops 7530872832 | bytes 33292288 | tf_op jit(solution)/shard_map/vt,td->vd/dot_general | solution.py:386
  107.3 0.0 copy-done
  107.3 0.0 collective-permute-done
  107.3 0.2 fusion.6
  107.5 0.0 copy-done.1
  107.5 0.2 fusion.2
  107.8 0.8 fusion.7
  (4 shorter events, 0.0 us)
Async XLA Ops:
  0.6 106.7 %collective-permute-start = (bf16[8,7168]{1,0:T(8,128)(2,1)}, bf16[8,7168]{1,0:T(8,128)(2,1)S(1)}, u32[]{:S(2)}, u32[]{:S(2)}) collective-permute-start(bf16[8,7168]{1,0:T(8,128)(2,1)} %bitcast.14), channel_id=1, source_target_pairs={{0,16},{16,0},{1,17},{17,1},{2,18},{18,2},{3,19},{19,3},{4,20},{20... | collective-permute-start | bytes 344072 | tf_op jit(solution)/shard_map/ppermute | solution.py:333
  92.4 14.9 %copy-start = (f32[2,7,8,512]{3,2,1,0:T(8,128)S(1)}, f32[2,7,8,512]{3,2,1,0:T(8,128)}, u32[]{:S(2)}) copy-start(f32[2,7,8,512]{3,2,1,0:T(8,128)} %get-tuple-element.5) | copy-start | bytes 688132
  92.4 15.1 %copy-start.1 = (f32[7168]{0:T(1024)S(1)}, f32[7168]{0:T(1024)}, u32[]{:S(2)}) copy-start(f32[7168]{0:T(1024)} %param.6) | copy-start | bytes 86020

commit v3 on v2

--- a/solution.py
+++ b/solution.py
@@ -18,6 +18,7 @@
 SLAB = 512
 SLOTS = 4
 TILE = 512
+ROWS = 256
 
 
 def fused_kernel(
@@ -322,6 +323,12 @@
 
     rows_copy.wait()
     grad_copy.wait()
+
+
+def weight_kernel(grad_ref, rows_ref, out_ref):
+    out_ref[...] = jnp.dot(
+        grad_ref[...], rows_ref[...], preferred_element_type=jnp.float32
+    ).astype(out_ref.dtype)
 
 
 def fused_plan(hidden, gain, table, labels, token_weight):
@@ -383,9 +390,17 @@
             flops=6 * tokens * vocab * width, bytes_accessed=3 * vocab * width, transcendentals=0
         ),
     )(hidden[0], gain[None], table, marks)
-    table_grad = jnp.einsum(
-        "vt,td->vd", grad_t, rows.reshape(2 * tokens, half), preferred_element_type=f32
-    ).astype(b16)
+    table_grad = pl.pallas_call(
+        weight_kernel,
+        grid=(vocab // ROWS,),
+        out_shape=jax.ShapeDtypeStruct((vocab, half), b16),
+        in_specs=[
+            pl.BlockSpec((ROWS, 2 * tokens), lambda i: (i, 0)),
+            pl.BlockSpec((2 * tokens, half), lambda i: (0, 0)),
+        ],
+        out_specs=pl.BlockSpec((ROWS, half), lambda i: (i, 0)),
+        compiler_params=pltpu.CompilerParams(vmem_limit_bytes=48 * 2**20),
+    )(grad_t, rows.reshape(2 * tokens, half))
     normed_grad = jnp.transpose(sums, (2, 1, 0, 3)).reshape(own, width)
     inverse, unit, _ = normalize(other_rows, gain)
     scaled = normed_grad * gain

time: 109 us -> 113 us (1.037)
  Pallas kernels: 86.7 us -> 102 us
  matrix products: 14.9 us -> 0 us
  local copies, waits for them, and re-layouts: 0.1 us -> 4.13 us
    pallas_call x0 -> x1, Pallas kernels: none -> 15.6 us  [fused_plan(): pl.pallas_call(weight_kernel, grid=(vocab // ROWS,), out_shape=jax.ShapeD...]
    dot_general x1 -> x0, matrix products: 14.9 us -> none  [fused_plan(): jnp.einsum('vt,td->vd', grad_t, rows.reshape(2 * tokens, half), preferred...]
    unnamed x4 -> x6, local copies, waits for them, and re-layouts: 0.01 us -> 3.09 us
  transfers between devices with their start and end apart: 1 -> 1, of which waited for: 0 -> 0; matrix products, arithmetic and copies ran while one was open for 16% -> 3% of each run, Pallas kernels for 80% -> 90%
where the time goes in v3:
time: 113 us
  Pallas kernels  102 us (90%)
  local copies, waits for them, and re-layouts  4.13 us (4%)
  other arithmetic  3.17 us (3%)
  starting transfers between devices  3 us (3%)
    pallas_call x1, Pallas kernels, fused_plan(): pl.pallas_call(fused_kernel, out_shape=(jax.ShapeDtypeStruct((vocab, 2 *...  86.7 us
    pallas_call x1, Pallas kernels, fused_plan(): pl.pallas_call(weight_kernel, grid=(vocab // ROWS,), out_shape=jax.ShapeD...  15.6 us
    unnamed x6, local copies, waits for them, and re-layouts  3.09 us
    ppermute x1, starting transfers between devices, fused_plan(): other_rows = lax.ppermute(hidden[0], 'section', [(0, 1), (1, 0)])  3 us
  transfers between devices with their start and end apart: 1, of which 0 were waited for; matrix products, arithmetic and copies ran while one was open for 3% of the time, Pallas kernels for 90%

profile of v3, /device:TPU:0, one launch (start us, length us, event | category | flops | bytes accessed | tf_op | source)
XLA Modules:
  0.0 113.3 jit_solution(2728685860648468975)
XLA Ops:
  0.6 3.0 %collective-permute-start = (bf16[8,7168]{1,0:T(8,128)(2,1)}, bf16[8,7168]{1,0:T(8,128)(2,1)S(1)}, u32[]{:S(2)}, u32[]{:S(2)}) collective-permute-start(bf16[8,7168]{1,0:T(8,128)(2,1)} %bitcast.12), channel_id=1, source_target_pairs={{0,16},{16,0},{1,17},{17,1},{2,18},{18,2},{3,19},{19,3},{4,20},{20... | collective-permute-start | bytes 344072 | tf_op jit(solution)/shard_map/ppermute | solution.py:340
  3.6 0.7 convert_element_type.10
  4.3 0.1 pad.2.clone
  4.4 1.3 %maximum_maximum_fusion.marks_ref = f32[8,128]{1,0:T(8,128)} fusion(f32[1,128]{1,0:T(1,128)} %param.9, f32[1,128]{1,0:T(1,128)S(1)} %convert_element_type.10, f32[8]{0:T(128)S(1)} %pad.2.clone), kind=kLoop, calls=%fused_computation.10 | loop fusion | flops 2048 | bytes 5152 | tf_op jit(solution)/shard_map/concatenate | solution.py:341
  5.7 86.7 %shard_map.68 = (bf16[4096,256]{1,0:T(8,128)(2,1)}, bf16[2,4,2,16,3584]{4,3,2,1,0:T(8,128)(2,1)}, f32[2,7,8,512]{3,2,1,0:T(8,128)}) custom-call(bf16[8,7168]{1,0:T(8,128)(2,1)} %bitcast.13, f32[1,7168]{1,0:T(1,128)} %bitcast.11, bf16[4096,7168]{1,0:T(8,128)(2,1)} %table_ref.1, f32[8,128]{1,0:T(8,128)} %maximum_maximum_fusion.marks_ref), custom_call_target="tpu_custom_call" | custom-call | flops 22548578304 | bytes 88080384 | tf_op jit(solution)/shard_map/pallas_call | solution.py:346
  92.4 0.0 copy-start.2
  92.4 1.0 copy.7
  93.3 0.0 copy-start
  93.4 1.6 %copy-done = bf16[4096,256]{1,0:T(8,128)(2,1)S(1)} copy-done((bf16[4096,256]{1,0:T(8,128)(2,1)S(1)}, bf16[4096,256]{1,0:T(8,128)(2,1)}, u32[]{:S(2)}) %copy-start) | copy-done | bytes 2097176
  94.9 0.0 copy-start.1
  94.9 1.5 %copy-done.1 = bf16[2,4,2,16,3584]{4,3,2,1,0:T(8,128)(2,1)S(1)} copy-done((bf16[2,4,2,16,3584]{4,3,2,1,0:T(8,128)(2,1)S(1)}, bf16[2,4,2,16,3584]{4,3,2,1,0:T(8,128)(2,1)}, u32[]{:S(2)}) %copy-start.1) | copy-done | bytes 1835032
  96.4 15.6 %shard_map.69 = bf16[4096,3584]{1,0:T(8,128)(2,1)} custom-call(bf16[4096,256]{1,0:T(8,128)(2,1)S(1)} %copy-done, bf16[256,3584]{1,0:T(8,128)(2,1)S(1)} %bitcast.7), custom_call_target="tpu_custom_call" | custom-call | tf_op jit(solution)/shard_map/pallas_call | solution.py:393
  112.0 0.0 collective-permute-done
  112.1 0.2 fusion.6
  112.2 0.0 copy-done.2
  112.2 0.2 fusion.2
  112.5 0.8 fusion.7
  (3 shorter events, 0.0 us)
Async XLA Ops:
  0.6 111.4 %collective-permute-start = (bf16[8,7168]{1,0:T(8,128)(2,1)}, bf16[8,7168]{1,0:T(8,128)(2,1)S(1)}, u32[]{:S(2)}, u32[]{:S(2)}) collective-permute-start(bf16[8,7168]{1,0:T(8,128)(2,1)} %bitcast.12), channel_id=1, source_target_pairs={{0,16},{16,0},{1,17},{17,1},{2,18},{18,2},{3,19},{19,3},{4,20},{20... | collective-permute-start | bytes 344072 | tf_op jit(solution)/shard_map/ppermute | solution.py:340
  92.4 19.9 %copy-start.2 = (f32[7168]{0:T(1024)S(1)}, f32[7168]{0:T(1024)}, u32[]{:S(2)}) copy-start(f32[7168]{0:T(1024)} %param.6) | copy-start | bytes 86020
  93.3 1.6 %copy-start = (bf16[4096,256]{1,0:T(8,128)(2,1)S(1)}, bf16[4096,256]{1,0:T(8,128)(2,1)}, u32[]{:S(2)}) copy-start(bf16[4096,256]{1,0:T(8,128)(2,1)} %get-tuple-element.6.grad_ref) | copy-start | bytes 6291460
  94.9 1.5 %copy-start.1 = (bf16[2,4,2,16,3584]{4,3,2,1,0:T(8,128)(2,1)S(1)}, bf16[2,4,2,16,3584]{4,3,2,1,0:T(8,128)(2,1)}, u32[]{:S(2)}) copy-start(bf16[2,4,2,16,3584]{4,3,2,1,0:T(8,128)(2,1)} %get-tuple-element.7) | copy-start | bytes 5505028
